TPU v7x, 512 devices: a whole 4x8x8 slice. The times are simulated.
512 devices in a mesh: seg: 32 (over x, y), bond: 16 (over z, core).
Axes of the slice: x: 4, y: 8, z: 8, core: 2. Of those that a mesh axis runs over, the one named last changes fastest.
Arguments:
- env_in: bfloat16 [32, 16, 512, 512], P('seg', 'bond'), may hold values from -6 to 6
- site: bfloat16 [32, 16, 2, 512, 512], P('seg', 'bond'), may hold values from -0.125 to 0.125
- right_env: bfloat16 [32, 16, 512, 512], P('seg', 'bond'), may hold values from -18 to 18
- comp_ids: int32 [32, 4], P('seg'), may hold values from 0 to 2
- counts: int32 [32], P('seg'), may hold values from 1 to 4, as said below
Outputs:
- env_out: float32 [32, 16, 512, 512], P('seg', 'bond')
- corr: float32 [32], P('seg')
Inputs may be any that keep to these rules, and one draw needn't show every extreme that they name: `counts`: some segment's list has length 4 in every draw.
All inputs are finite; a program needn't handle non-finite values.
Results may differ from a plain program's by a relative error of at most 0.00055.
Values may be sent and summed in bfloat16 or wider, within the bound.
A program may use at most 64 MiB of HBM per device.

v0:
```python
import math

import jax
import jax.numpy as jnp
from jax import lax
from jax.sharding import PartitionSpec as P


def swapped(array, axis, apart):
    return lax.ppermute(array, axis, [(i, i ^ 1 << apart) for i in range(lax.axis_size(axis))])


def from_behind(array, axis, by):
    peers = lax.axis_size(axis)
    pairs = [(i, i + by) for i in range(peers) if 0 <= i + by < peers]
    return lax.ppermute(array, axis, pairs)


def spin_table():
    return jnp.array(
        [[[0.5, 0.0], [0.0, -0.5]], [[0.0, 0.5], [0.5, 0.0]], [[0.0, 0.5], [-0.5, 0.0]]],
        jnp.float32,
    )


def local_operator(ids_row, count_now):
    active = jnp.arange(ids_row.shape[0], dtype=jnp.int32) < count_now
    matches = (ids_row[:, None] == jnp.arange(3, dtype=jnp.int32)[None, :]).astype(jnp.float32)
    tallies = jnp.sum(jnp.where(active[:, None], matches, jnp.zeros_like(matches)), axis=0)
    return jnp.einsum("c,cst->st", tallies, spin_table())


def body(env_in, site, right_env, comp_ids, counts):
    grid_side = math.isqrt(lax.axis_size("bond"))
    levels = grid_side.bit_length() - 1
    bond_index = lax.axis_index("bond")
    env_tile = env_in[0, 0]
    site_tile = site[0, 0]
    tile_size = env_tile.shape[0]
    bond_dim = grid_side * tile_size
    highest = lax.Precision.HIGHEST
    env_strip = env_tile
    for bit_pos in range(levels):
        partner = swapped(env_strip, "bond", bit_pos)
        upper_half = bond_index >> bit_pos & 1 == 1
        env_strip = jnp.where(
            upper_half,
            jnp.concatenate([partner, env_strip], axis=1),
            jnp.concatenate([env_strip, partner], axis=1),
        )
    column_strip = site_tile
    for bit_pos in range(levels):
        partner = swapped(column_strip, "bond", levels + bit_pos)
        upper_half = bond_index >> levels + bit_pos & 1 == 1
        column_strip = jnp.where(
            upper_half,
            jnp.concatenate([partner, column_strip], axis=1),
            jnp.concatenate([column_strip, partner], axis=1),
        )
    operator = local_operator(comp_ids[0], counts[0])
    product = jnp.einsum("ak,skb->sab", env_strip, column_strip, preferred_element_type=jnp.float32)
    weighted = jnp.einsum("st,tab->sab", operator, product, precision=highest)
    row_strip = site_tile
    for bit_pos in range(levels):
        partner = swapped(row_strip, "bond", bit_pos)
        upper_half = bond_index >> bit_pos & 1 == 1
        row_strip = jnp.where(
            upper_half,
            jnp.concatenate([partner, row_strip], axis=2),
            jnp.concatenate([row_strip, partner], axis=2),
        )
    partials = jnp.einsum("sar,sab->rb", row_strip.astype(jnp.float32), weighted, precision=highest)
    partials = partials.reshape(grid_side, tile_size, tile_size)
    for level in reversed(range(levels)):
        half_count = partials.shape[0] // 2
        lower_half = partials[:half_count]
        upper_part = partials[half_count:]
        mine_upper = bond_index >> levels + level & 1 == 1
        kept_half = jnp.where(mine_upper, upper_part, lower_half)
        sent_half = jnp.where(mine_upper, lower_half, upper_part)
        received = swapped(sent_half, "bond", levels + level)
        partials = kept_half + received
    pushed = partials.reshape(tile_size, tile_size)
    right_tile = right_env[0, 0]
    arrived = from_behind(pushed, "seg", 1)
    term = jnp.sum(arrived * right_tile.astype(jnp.float32))
    closed = lax.psum(term, "bond") / bond_dim
    return (pushed.reshape(1, 1, tile_size, tile_size), closed.reshape(1))


def solution(mesh):
    placed = (
        P("seg", "bond", None, None),
        P("seg", "bond", None, None, None),
        P("seg", "bond", None, None),
        P("seg", None),
        P("seg"),
    )
    return jax.shard_map(
        body,
        mesh=mesh,
        in_specs=placed,
        out_specs=(P("seg", "bond", None, None), P("seg")),
        check_vma=False,
    )
```

profile of v0, /device:TPU:7, one launch (start us, length us, event | category | flops | bytes accessed | tf_op | source)
XLA Modules:
  0.0 436.5 jit_solution(13097608077848003396)
XLA Ops:
  0.6 5.8 %collective-permute-start.2 = (bf16[2,512,512]{2,1,0:T(8,128)(2,1)}, bf16[2,512,512]{2,1,0:T(8,128)(2,1)S(1)}, u32[]{:S(2)}, u32[]{:S(2)}) collective-permute-start(bf16[2,512,512]{2,1,0:T(8,128)(2,1)} %bitcast.32), channel_id=1, source_target_pairs={{0,4},{1,5},{2,6},{3,7},{4,0},{5,1},{6,2},{7,3},{8,12},{9,13},{10,... | collective-permute-start | bytes 3145736 | tf_op jit(solution)/shard_map/ppermute | solution.py:10
  6.4 2.9 collective-permute-start
  9.3 42.7 %collective-permute-done.2 = bf16[2,512,512]{2,1,0:T(8,128)(2,1)S(1)} collective-permute-done((bf16[2,512,512]{2,1,0:T(8,128)(2,1)}, bf16[2,512,512]{2,1,0:T(8,128)(2,1)S(1)}, u32[]{:S(2)}, u32[]{:S(2)}) %collective-permute-start.2) | collective-permute-done | bytes 1048608 | tf_op jit(solution)/shard_map/ppermute | solution.py:10
  52.0 2.1 maximum_select_fusion.7
  54.1 9.0 %collective-permute-start.3 = (bf16[2,1024,512]{2,1,0:T(8,128)(2,1)S(1)}, bf16[2,1024,512]{2,1,0:T(8,128)(2,1)}, u32[]{:S(2)}, u32[]{:S(2)}) collective-permute-start(bf16[2,1024,512]{2,1,0:T(8,128)(2,1)S(1)} %maximum_select_fusion.7), channel_id=1, source_target_pairs={{0,8},{1,9},{2,10},{3,11},{4,12},{5,13},{6,14},{7,15},{8,0},{9,1},... | collective-permute-start | bytes 6291464 | tf_op jit(solution)/shard_map/ppermute | solution.py:10
  63.2 3.6 collective-permute-start.4
  66.8 1.9 collective-permute-done.4
  68.7 2.9 maximum_select_fusion.11
  71.5 2.3 collective-permute-start.5
  73.9 3.6 maximum_select_fusion.6
  77.5 3.1 collective-permute-start.1
  81.2 0.1 select_reduce_fusion
  81.3 0.1 fusion.28
  81.5 95.9 %collective-permute-done.5 = bf16[512,1024]{1,0:T(8,128)(2,1)} collective-permute-done((bf16[512,1024]{1,0:T(8,128)(2,1)}, bf16[512,1024]{1,0:T(8,128)(2,1)}, u32[]{:S(2)}, u32[]{:S(2)}) %collective-permute-start.5) | collective-permute-done | bytes 1048608 | tf_op jit(solution)/shard_map/ppermute | solution.py:10
  177.4 7.3 %fusion.24 = f32[2,512,512]{1,2,0:T(8,128)} fusion(bf16[512,1024]{1,0:T(8,128)(2,1)} %maximum_select_fusion.11, bf16[512,1024]{1,0:T(8,128)(2,1)} %collective-permute-done.5, pred[]{:T(512)S(6)} %eq.33, bf16[2,1024,512]{2,1,0:T(8,128)(2,1)S(1)} %maximum_select_fusion.7, bf16[2,1024,512]{2,1,0:T(8,128)(2,1)} %collective-permute-done.3, pred[]{:T(512)S(6)} %eq.32), kind=kOutput, calls=%fused_computation.30 | convolution fusion | flops 2175795200 | bytes 8388610 | tf_op jit(solution)/shard_map/ak,skb->sab/dot_general | solution.py:61
  184.7 2.9 copy.12
  187.6 7.6 %fusion.32 = f32[2,512,512]{2,0,1:T(2,128)S(1)} fusion(f32[2,2,1]{1,0,2:T(2,128)S(1)} %bitcast.39, f32[2,512,512]{2,0,1:T(2,128)S(1)} %copy.12), kind=kOutput, calls=%fused_computation.43 | convolution fusion | flops 12582912 | bytes 4194320 | tf_op jit(solution)/shard_map/st,tab->sab/dot_general | solution.py:62
  195.1 27.1 %collective-permute-done.1 = bf16[2,512,1024]{2,1,0:T(8,128)(2,1)} collective-permute-done((bf16[2,512,1024]{2,1,0:T(8,128)(2,1)}, bf16[2,512,1024]{2,1,0:T(8,128)(2,1)}, u32[]{:S(2)}, u32[]{:S(2)}) %collective-permute-start.1) | collective-permute-done | bytes 2097184 | tf_op jit(solution)/shard_map/ppermute | solution.py:10
  222.3 11.6 %fusion.14 = f32[2048,512]{1,0:T(8,128)S(1)} fusion(bf16[2,512,1024]{2,1,0:T(8,128)(2,1)} %maximum_select_fusion.6, bf16[2,512,1024]{2,1,0:T(8,128)(2,1)} %collective-permute-done.1, pred[]{:T(512)S(6)} %eq.33, f32[2,512,512]{2,0,1:T(2,128)S(1)} %fusion.32), kind=kOutput, calls=%fused_computation.16 | convolution fusion | flops 12903776256 | bytes 10485761 | tf_op jit(solution)/shard_map/sar,sab->rb/dot_general | solution.py:72
  233.9 0.6 slice_select_fusion
  234.5 2.5 collective-permute-start.6
  237.0 82.1 %collective-permute-done.6 = f32[2,512,512]{2,1,0:T(8,128)S(1)} collective-permute-done((f32[2,512,512]{2,1,0:T(8,128)S(1)}, f32[2,512,512]{2,1,0:T(8,128)S(1)}, u32[]{:S(2)}, u32[]{:S(2)}) %collective-permute-start.6) | collective-permute-done | bytes 2097184 | tf_op jit(solution)/shard_map/ppermute | solution.py:10
  319.1 0.5 add.8
  319.6 0.2 slice_select_fusion.2
  319.8 0.0 copy-start.2
  319.8 14.6 %collective-permute-start.7 = (f32[1,512,512]{2,1,0:T(8,128)S(1)}, f32[1,512,512]{2,1,0:T(8,128)S(1)}, u32[]{:S(2)}, u32[]{:S(2)}) collective-permute-start(f32[1,512,512]{2,1,0:T(8,128)S(1)} %slice_select_fusion.2), channel_id=1, source_target_pairs={{0,4},{1,5},{2,6},{3,7},{4,0},{5,1},{6,2},{7,3},{8,12},{9,13},{10,... | collective-permute-start | bytes 3145736 | tf_op jit(solution)/shard_map/ppermute | solution.py:10
  334.4 46.0 %collective-permute-done.7 = f32[1,512,512]{2,1,0:T(8,128)S(1)} collective-permute-done((f32[1,512,512]{2,1,0:T(8,128)S(1)}, f32[1,512,512]{2,1,0:T(8,128)S(1)}, u32[]{:S(2)}, u32[]{:S(2)}) %collective-permute-start.7) | collective-permute-done | bytes 1048608 | tf_op jit(solution)/shard_map/ppermute | solution.py:10
  380.4 0.4 select_add_fusion
  380.7 3.2 collective-permute-start.8
  384.0 24.9 %collective-permute-done.8 = f32[512,512]{1,0:T(8,128)S(1)} collective-permute-done((f32[512,512]{1,0:T(8,128)S(1)}, f32[512,512]{1,0:T(8,128)S(1)}, u32[]{:S(2)}, u32[]{:S(2)}) %collective-permute-start.8) | collective-permute-done | bytes 1048608 | tf_op jit(solution)/shard_map/ppermute | solution.py:16
  408.9 0.9 fusion.27
  409.8 25.0 %psum.7 = f32[]{:T(128)} all-reduce(f32[]{:T(128)} %fusion.27), channel_id=1, replica_groups=mesh['seg'=32,'bond'=16] {'bond'}, use_global_device_ids=true, to_apply=%region_2.3 | all-reduce | flops 1 | bytes 8 | tf_op jit(solution)/shard_map/psum | solution.py:87
  (12 shorter events, 0.0 us)
Async XLA Ops:
  0.6 51.4 %collective-permute-start.2 = (bf16[2,512,512]{2,1,0:T(8,128)(2,1)}, bf16[2,512,512]{2,1,0:T(8,128)(2,1)S(1)}, u32[]{:S(2)}, u32[]{:S(2)}) collective-permute-start(bf16[2,512,512]{2,1,0:T(8,128)(2,1)} %bitcast.32), channel_id=1, source_target_pairs={{0,4},{1,5},{2,6},{3,7},{4,0},{5,1},{6,2},{7,3},{8,12},{9,13},{10,... | collective-permute-start | bytes 3145736 | tf_op jit(solution)/shard_map/ppermute | solution.py:10
  6.4 67.4 %collective-permute-start = (bf16[2,512,512]{2,1,0:T(8,128)(2,1)}, bf16[2,512,512]{2,1,0:T(8,128)(2,1)}, u32[]{:S(2)}, u32[]{:S(2)}) collective-permute-start(bf16[2,512,512]{2,1,0:T(8,128)(2,1)} %bitcast.33), channel_id=1, source_target_pairs={{0,1},{1,0},{2,3},{3,2},{4,5},{5,4},{6,7},{7,6},{8,9},{9,8},{10,11... | collective-permute-start | bytes 3145736 | tf_op jit(solution)/shard_map/ppermute | solution.py:10
  54.1 19.7 %copy-start = (bf16[1,1,2,512,512]{4,3,2,1,0:T(8,128)(2,1)S(1)}, bf16[1,1,2,512,512]{4,3,2,1,0:T(8,128)(2,1)}, u32[]{:S(2)}) copy-start(bf16[1,1,2,512,512]{4,3,2,1,0:T(8,128)(2,1)} %param.7) | copy-start | bytes 3145732
  54.1 123.2 %collective-permute-start.3 = (bf16[2,1024,512]{2,1,0:T(8,128)(2,1)S(1)}, bf16[2,1024,512]{2,1,0:T(8,128)(2,1)}, u32[]{:S(2)}, u32[]{:S(2)}) collective-permute-start(bf16[2,1024,512]{2,1,0:T(8,128)(2,1)S(1)} %maximum_select_fusion.7), channel_id=1, source_target_pairs={{0,8},{1,9},{2,10},{3,11},{4,12},{5,13},{6,14},{7,15},{8,0},{9,1},... | collective-permute-start | bytes 6291464 | tf_op jit(solution)/shard_map/ppermute | solution.py:10
  63.2 5.5 %collective-permute-start.4 = (bf16[512,512]{1,0:T(8,128)(2,1)}, bf16[512,512]{1,0:T(8,128)(2,1)}, u32[]{:S(2)}, u32[]{:S(2)}) collective-permute-start(bf16[512,512]{1,0:T(8,128)(2,1)} %bitcast.7), channel_id=1, source_target_pairs={{0,1},{1,0},{2,3},{3,2},{4,5},{5,4},{6,7},{7,6},{8,9},{9,8},{10,11... | collective-permute-start | bytes 1572872 | tf_op jit(solution)/shard_map/ppermute | solution.py:10
  71.5 9.7 %copy-start.3 = (s32[1,4]{1,0:T(1,128)S(1)}, s32[1,4]{1,0:T(1,128)}, u32[]{:S(2)}) copy-start(s32[1,4]{1,0:T(1,128)} %param.9) | copy-start | bytes 52
  71.5 9.8 %copy-start.4 = (bf16[3,2,2]{0,2,1:T(2,128)(2,1)S(1)}, bf16[3,2,2]{0,2,1:T(2,128)(2,1)}, u32[]{:S(2)}) copy-start(bf16[3,2,2]{0,2,1:T(2,128)(2,1)} %constant.78) | copy-start | bytes 76
  71.5 105.8 %collective-permute-start.5 = (bf16[512,1024]{1,0:T(8,128)(2,1)}, bf16[512,1024]{1,0:T(8,128)(2,1)}, u32[]{:S(2)}, u32[]{:S(2)}) collective-permute-start(bf16[512,1024]{1,0:T(8,128)(2,1)} %maximum_select_fusion.11), channel_id=1, source_target_pairs={{0,2},{1,3},{2,0},{3,1},{4,6},{5,7},{6,4},{7,5},{8,10},{9,11},{10,... | collective-permute-start | bytes 3145736 | tf_op jit(solution)/shard_map/ppermute | solution.py:10
  77.5 144.8 %collective-permute-start.1 = (bf16[2,512,1024]{2,1,0:T(8,128)(2,1)}, bf16[2,512,1024]{2,1,0:T(8,128)(2,1)}, u32[]{:S(2)}, u32[]{:S(2)}) collective-permute-start(bf16[2,512,1024]{2,1,0:T(8,128)(2,1)} %maximum_select_fusion.6), channel_id=1, source_target_pairs={{0,2},{1,3},{2,0},{3,1},{4,6},{5,7},{6,4},{7,5},{8,10},{9,11},{10,... | collective-permute-start | bytes 6291464 | tf_op jit(solution)/shard_map/ppermute | solution.py:10
  234.5 84.6 %collective-permute-start.6 = (f32[2,512,512]{2,1,0:T(8,128)S(1)}, f32[2,512,512]{2,1,0:T(8,128)S(1)}, u32[]{:S(2)}, u32[]{:S(2)}) collective-permute-start(f32[2,512,512]{2,1,0:T(8,128)S(1)} %bitcast.36), channel_id=1, source_target_pairs={{0,8},{1,9},{2,10},{3,11},{4,12},{5,13},{6,14},{7,15},{8,0},{9,1},... | collective-permute-start | bytes 6291464 | tf_op jit(solution)/shard_map/ppermute | solution.py:10
  319.8 89.1 %copy-start.2 = (bf16[1,1,512,512]{3,2,1,0:T(8,128)(2,1)S(1)}, bf16[1,1,512,512]{3,2,1,0:T(8,128)(2,1)}, u32[]{:S(2)}) copy-start(bf16[1,1,512,512]{3,2,1,0:T(8,128)(2,1)} %param.8) | copy-start | bytes 1572868
  319.8 60.6 %collective-permute-start.7 = (f32[1,512,512]{2,1,0:T(8,128)S(1)}, f32[1,512,512]{2,1,0:T(8,128)S(1)}, u32[]{:S(2)}, u32[]{:S(2)}) collective-permute-start(f32[1,512,512]{2,1,0:T(8,128)S(1)} %slice_select_fusion.2), channel_id=1, source_target_pairs={{0,4},{1,5},{2,6},{3,7},{4,0},{5,1},{6,2},{7,3},{8,12},{9,13},{10,... | collective-permute-start | bytes 3145736 | tf_op jit(solution)/shard_map/ppermute | solution.py:10
  380.7 54.7 %copy-start.1 = (f32[1,512,512]{2,1,0:T(8,128)}, f32[1,512,512]{2,1,0:T(8,128)S(1)}, u32[]{:S(2)}) copy-start(f32[1,512,512]{2,1,0:T(8,128)S(1)} %select_add_fusion) | copy-start | bytes 3145732
  380.7 28.1 %collective-permute-start.8 = (f32[512,512]{1,0:T(8,128)S(1)}, f32[512,512]{1,0:T(8,128)S(1)}, u32[]{:S(2)}, u32[]{:S(2)}) collective-permute-start(f32[512,512]{1,0:T(8,128)S(1)} %bitcast.37), channel_id=1, source_target_pairs={{0,16},{16,32},{32,48},{48,64},{64,80},{80,96},{96,112},{112,128},... | collective-permute-start | bytes 3145736 | tf_op jit(solution)/shard_map/ppermute | solution.py:16
where the time goes:
time: 437 us
  waiting for transfers between devices  321 us (73%)
  starting transfers between devices  47 us (11%)
  matrix products  26.7 us (6%)
  blocking collectives  25 us (6%)
  other arithmetic  11.2 us (3%)
    ppermute x8, waiting for transfers between devices, swapped(): lax.ppermute(array, axis, [(i, i ^ 1 << apart) for i in range(lax.axis_si...  296 us
    ppermute x8, starting transfers between devices, swapped(): lax.ppermute(array, axis, [(i, i ^ 1 << apart) for i in range(lax.axis_si...  43.8 us
    psum x1, blocking collectives, body(): closed = lax.psum(term, 'bond') / bond_dim  25 us
    ppermute x1, waiting for transfers between devices, from_behind(): return lax.ppermute(array, axis, pairs)  24.9 us
    dot_general x1, matrix products, body(): jnp.einsum('sar,sab->rb', row_strip.astype(jnp.float32), weighted, precis...  11.6 us
  transfers between devices with their start and end apart: 9, of which 7 were waited for; matrix products, arithmetic and copies ran while one was open for 6% of the time, Pallas kernels for 0%

commit v1 on v0

v1 whole, which is shorter than its diff:
```python
import functools
import math

import jax
import jax.numpy as jnp
from jax import lax
from jax.experimental import pallas as pl
from jax.experimental.pallas import tpu as pltpu
from jax.sharding import PartitionSpec as P

MESH = pl.DeviceIdType.MESH
F32 = jnp.float32
BF16 = jnp.bfloat16


def kernel(
    side, bonds, segs,
    ids, counts, env, site, right,
    out, corr,
    e_all, a_all, w_acc, out_acc, right_in, term, terms_in,
    ring_send, ring_recv, e_send, e_recv, a_send, a_recv,
    right_send, right_recv, term_send, term_recv, local_sem,
):
    chips = bonds // 2
    seg = lax.axis_index("seg")
    bond = lax.axis_index("bond")
    z = bond // 2
    core = bond % 2
    row = bond // side
    column = bond % side
    half = z % 2
    turn = 1 - 2 * core

    def chip_at(step):
        return (z - turn * step + 2 * chips) % chips

    def mirrored(step):
        return (z + turn * step + 2 * chips) % chips

    def steps_from(chip, own_core):
        towards = jnp.where(own_core, z - chip, chip - z)
        return (towards * turn + 2 * chips) % chips

    following = (seg, ((z + turn + chips) % chips) * 2 + core)
    previous = (seg, ((z - turn + chips) % chips) * 2 + core)
    sibling = (seg, z * 2 + 1 - core)
    has_before = seg > 0
    has_after = seg < segs - 1

    barrier = pltpu.get_barrier_semaphore()
    pl.semaphore_signal(barrier, inc=1, device_id=previous, device_id_type=MESH)
    pl.semaphore_signal(barrier, inc=1, device_id=sibling, device_id_type=MESH)

    @pl.when(has_after)
    def _():
        pl.semaphore_signal(barrier, inc=1, device_id=(seg + 1, bond), device_id_type=MESH)

    @pl.when(has_before)
    def _():
        for peer in range(bonds):
            pl.semaphore_signal(barrier, inc=1, device_id=(seg - 1, peer), device_id_type=MESH)

    own_env = pltpu.make_async_copy(env.at[0, 0], e_all.at[bond], local_sem.at[0])
    own_site = pltpu.make_async_copy(site.at[0, 0], a_all.at[z], local_sem.at[1])
    own_env.start()
    own_site.start()
    w_acc[...] = jnp.zeros_like(w_acc)
    out_acc[...] = jnp.zeros_like(out_acc)

    pl.semaphore_wait(barrier, 2 + jnp.where(has_before, 1, 0) + jnp.where(has_after, bonds, 0))

    def ring_copy(step, part):
        chip = chip_at(step)
        if part == 0:
            ref = e_all.at[chip * 2 + core]
        else:
            ref = a_all.at[chip, part - 1]
        return pltpu.make_async_remote_copy(
            src_ref=ref, dst_ref=ref,
            send_sem=ring_send.at[step * 3 + part], recv_sem=ring_recv.at[step * 3 + part],
            device_id=following, device_id_type=MESH,
        )

    def ring_arrival(step, part):
        chip = chip_at(step)
        if part == 0:
            ref = e_all.at[chip * 2 + core]
        else:
            ref = a_all.at[chip, part - 1]
        return pltpu.make_async_remote_copy(
            src_ref=ref, dst_ref=ref,
            send_sem=ring_send.at[(step - 1) * 3 + part], recv_sem=ring_recv.at[(step - 1) * 3 + part],
            device_id=following, device_id_type=MESH,
        )

    def env_across(step, chip, at_core):
        ref = e_all.at[chip * 2 + at_core]
        return pltpu.make_async_remote_copy(
            src_ref=ref, dst_ref=ref, send_sem=e_send.at[step], recv_sem=e_recv.at[step],
            device_id=sibling, device_id_type=MESH,
        )

    def site_across(chip):
        return pltpu.make_async_remote_copy(
            src_ref=a_all.at[chip], dst_ref=a_all.at[chips + chip // 2],
            send_sem=a_send.at[chip // 2], recv_sem=a_recv.at[chip // 2],
            device_id=sibling, device_id_type=MESH,
        )

    def column_of(chip, at_core):
        return 2 * (chip % 2) + at_core

    def site_goes_on(step):
        target = (z + turn + chips) % chips
        return (step < chips - 2) | ((step == chips - 2) & (target // 2 == column_of(chip_at(step), core)))

    def site_comes(step):
        return (step < chips - 1) | ((step == chips - 1) & (row == column_of(chip_at(step), core)))

    own_env.wait()
    ring_copy(0, 0).start()
    own_site.wait()
    ring_copy(0, 1).start()
    ring_copy(0, 2).start()
    env_across(0, z, core).start()

    @pl.when(column_of(z, core) == row)
    def _():
        site_across(z).start()

    @pl.when(has_before)
    def _():
        pltpu.make_async_remote_copy(
            src_ref=right.at[0, 0], dst_ref=right_in, send_sem=right_send, recv_sem=right_recv,
            device_id=(seg - 1, bond), device_id_type=MESH,
        ).start()

    tally = [jnp.float32(0.0)] * 3
    for k in range(ids.shape[1]):
        for c in range(3):
            tally[c] = tally[c] + jnp.where((k < counts[0]) & (ids[0, k] == c), jnp.float32(1.0), jnp.float32(0.0))
    half_z = 0.5 * tally[0]
    operator = ((half_z, 0.5 * tally[1] + 0.5 * tally[2]), (0.5 * tally[1] - 0.5 * tally[2], -half_z))

    def env_step(a, k):
        return steps_from(2 * a + k // 2, k % 2 == core)

    def site_step(k):
        return steps_from(2 * k + half, jnp.bool_(True))

    def left_step(a):
        return steps_from(2 * a + row // 2, row % 2 == core)

    def compute(step):
        def first(i, carry):
            a = i // side
            k = i % side

            @pl.when(jnp.maximum(env_step(a, k), site_step(k)) == step)
            def _():
                block = e_all[a * side + k]
                for t in range(2):
                    w_acc[a, t] += jnp.dot(block, a_all[2 * k + half, t], preferred_element_type=F32)

            return carry

        lax.fori_loop(0, side * side, first, 0)

        def second(a, carry):
            latest = left_step(a)
            for k in range(side):
                latest = jnp.maximum(latest, jnp.maximum(env_step(a, k), site_step(k)))

            @pl.when(latest == step)
            def _():
                slot = jnp.where(row % 2 == core, 2 * a + row // 2, chips + a)
                for s in range(2):
                    weighted = operator[s][0] * w_acc[a, 0] + operator[s][1] * w_acc[a, 1]
                    high = weighted.astype(BF16)
                    low = (weighted - high.astype(F32)).astype(BF16)
                    left = a_all[slot, s]
                    dims = (((0,), (0,)), ((), ()))
                    out_acc[...] += lax.dot_general(left, high, dims, preferred_element_type=F32)
                    out_acc[...] += lax.dot_general(left, low, dims, preferred_element_type=F32)

            return carry

        lax.fori_loop(0, side, second, 0)

    def across_arrivals(step):
        chip = mirrored(step)
        env_across(step, chip, 1 - core).wait_recv()

        @pl.when((row % 2 != core) & (column_of(chip, 1 - core) == row))
        def _():
            site_across(chip).wait_recv()

    across_arrivals(0)
    compute(0)

    def turn_of(step, carry):
        ring_arrival(step, 0).wait_recv()

        @pl.when(step < chips - 1)
        def _():
            ring_copy(step, 0).start()

        env_across(step, chip_at(step), core).start()

        @pl.when(site_comes(step))
        def _():
            for part in (1, 2):
                ring_arrival(step, part).wait_recv()

                @pl.when(site_goes_on(step))
                def _():
                    ring_copy(step, part).start()

            @pl.when(column_of(chip_at(step), core) == row)
            def _():
                site_across(chip_at(step)).start()

        across_arrivals(step)
        compute(step)
        return carry

    lax.fori_loop(1, chips, turn_of, 0)

    store = pltpu.make_async_copy(out_acc, out.at[0, 0], local_sem.at[2])
    store.start()

    @pl.when(has_after)
    def _():
        pltpu.make_async_remote_copy(
            src_ref=right.at[0, 0], dst_ref=right_in, send_sem=right_send, recv_sem=right_recv,
            device_id=(seg, bond), device_id_type=MESH,
        ).wait_recv()
        size = out_acc.shape[0]
        products = out_acc[...] * right_in[...].astype(F32)
        folded = jnp.sum(products.reshape(size // 8, 8, size), axis=0)
        total = folded[:, :128]
        for at in range(128, size, 128):
            total = total + folded[:, at : at + 128]
        term[...] = total
        for peer in range(bonds):
            pltpu.make_async_remote_copy(
                src_ref=term, dst_ref=terms_in.at[bond], send_sem=term_send.at[peer], recv_sem=term_recv,
                device_id=(seg + 1, peer), device_id_type=MESH,
            ).start()

    corr[0] = jnp.float32(0.0)

    @pl.when(has_before)
    def _():
        pltpu.make_async_remote_copy(
            src_ref=terms_in, dst_ref=terms_in, send_sem=term_send.at[0], recv_sem=term_recv,
            device_id=(seg, bond), device_id_type=MESH,
        ).wait_recv()
        size = out_acc.shape[0] * side
        corr[0] = jnp.sum(terms_in[...]) * (1.0 / size)
        pltpu.make_async_remote_copy(
            src_ref=right.at[0, 0], dst_ref=right_in, send_sem=right_send, recv_sem=right_recv,
            device_id=(seg, bond), device_id_type=MESH,
        ).wait_send()

    @pl.when(has_after)
    def _():
        for peer in range(bonds):
            pltpu.make_async_remote_copy(
                src_ref=term, dst_ref=terms_in.at[bond], send_sem=term_send.at[peer], recv_sem=term_recv,
                device_id=(seg, bond), device_id_type=MESH,
            ).wait_send()

    def drain(step, carry):
        @pl.when(step < chips - 1)
        def _():
            ring_copy(step, 0).wait_send()

            @pl.when(site_goes_on(step))
            def _():
                ring_copy(step, 1).wait_send()
                ring_copy(step, 2).wait_send()

        env_across(step, chip_at(step), core).wait_send()

        @pl.when(column_of(chip_at(step), core) == row)
        def _():
            site_across(chip_at(step)).wait_send()

        return carry

    lax.fori_loop(0, chips, drain, 0)
    store.wait()


def body(env_in, site, right_env, comp_ids, counts):
    bonds = lax.axis_size("bond")
    segs = lax.axis_size("seg")
    side = math.isqrt(bonds)
    chips = bonds // 2
    size = env_in.shape[-1]
    hbm = pl.BlockSpec(memory_space=pl.ANY)
    smem = pl.BlockSpec(memory_space=pltpu.SMEM)
    dma = pltpu.SemaphoreType.DMA
    return pl.pallas_call(
        functools.partial(kernel, side, bonds, segs),
        out_shape=(
            jax.ShapeDtypeStruct((1, 1, size, size), F32),
            jax.ShapeDtypeStruct((1,), F32),
        ),
        in_specs=[smem, smem, hbm, hbm, hbm],
        out_specs=(hbm, smem),
        scratch_shapes=[
            pltpu.VMEM((bonds, size, size), BF16),
            pltpu.VMEM((chips + side, 2, size, size), BF16),
            pltpu.VMEM((side, 2, size, size), F32),
            pltpu.VMEM((size, size), F32),
            pltpu.VMEM((size, size), BF16),
            pltpu.VMEM((8, 128), F32),
            pltpu.VMEM((bonds, 8, 128), F32),
            dma((3 * (chips - 1),)),
            dma((3 * (chips - 1),)),
            dma((chips,)),
            dma((chips,)),
            dma((side,)),
            dma((side,)),
            dma,
            dma,
            dma((bonds,)),
            dma,
            dma((3,)),
        ],
        compiler_params=pltpu.CompilerParams(
            collective_id=0, has_side_effects=True, vmem_limit_bytes=56 * 2**20
        ),
        cost_estimate=pl.CostEstimate(flops=26 * 10**9, bytes_accessed=6 * 2**20, transcendentals=0),
    )(comp_ids, counts, env_in, site, right_env)


def solution(mesh):
    placed = (
        P("seg", "bond", None, None),
        P("seg", "bond", None, None, None),
        P("seg", "bond", None, None),
        P("seg", None),
        P("seg"),
    )
    return jax.shard_map(
        body,
        mesh=mesh,
        in_specs=placed,
        out_specs=(P("seg", "bond", None, None), P("seg")),
        check_vma=False,
    )
```

time: 437 us -> 155 us (0.35)
  waiting for transfers between devices: 321 us -> 0 us
  Pallas kernels: 0 us -> 149 us
  starting transfers between devices: 47 us -> 0 us
  matrix products: 26.7 us -> 0 us
  blocking collectives: 25 us -> 0 us
  other arithmetic: 11.2 us -> 0 us
    ppermute x9 -> x0, waiting for transfers between devices: 321 us -> none  [the longest x8 296 us: swapped(): lax.ppermute(array, axis, [(i, i ^ 1 << apart) for i in range(lax.axis_si...]
    pallas_call x0 -> x1, Pallas kernels: none -> 149 us  [body(): pl.pallas_call(functools.partial(kernel, side, bonds, segs), out_shape=(j...]
    ppermute x9 -> x0, starting transfers between devices: 47 us -> none  [the longest x8 43.8 us: swapped(): lax.ppermute(array, axis, [(i, i ^ 1 << apart) for i in range(lax.axis_si...]
    dot_general x4 -> x0, matrix products: 26.7 us -> none  [the longest x1 11.6 us: body(): jnp.einsum('sar,sab->rb', row_strip.astype(jnp.float32), weighted, precis...]
    psum x1 -> x0, blocking collectives: 25 us -> none  [body(): closed = lax.psum(term, 'bond') / bond_dim]
    select_n x5 -> x0, other arithmetic: 9.37 us -> none  [the longest x1 3.6 us: body(): jnp.where(upper_half, jnp.concatenate([partner, row_strip], axis=2), jnp....]
  transfers between devices with their start and end apart: 9 -> 0, of which waited for: 7 -> 0; matrix products, arithmetic and copies ran while one was open for 6% -> 0% of each run, Pallas kernels for 0% -> 0%
where the time goes in v1:
time: 155 us; the launch traced here: 154 us
  Pallas kernels  149 us (96%)
  between operations  2.97 us (2%)
  local copies, waits for them, and re-layouts  2.26 us (1%)
    pallas_call x1, Pallas kernels, body(): pl.pallas_call(functools.partial(kernel, side, bonds, segs), out_shape=(j...  149 us

profile of v1, /device:TPU:7, one launch (start us, length us, event | category | flops | bytes accessed | tf_op | source)
XLA Modules:
  0.0 154.4 jit_solution(8902413613281046571)
XLA Ops:
  1.3 149.1 %shard_map.68 = (f32[1,1,512,512]{3,2,1,0:T(8,128)}, f32[1]{0:T(128)}) custom-call(s32[1,4]{1,0:T(1,128)} %ids.1, s32[1]{0:T(128)S(6)} %copy.9.counts, bf16[1,1,512,512]{3,2,1,0:T(8,128)(2,1)} %env.1, bf16[1,1,2,512,512]{4,3,2,1,0:T(8,128)(2,1)} %site.1, bf16[1,1,512,512]{3,2,1,0:T(8,128)(2,1)} %right.1), custom_call_target="tpu_custom_call" | custom-call | flops 25999998976 | bytes 6291456 | tf_op jit(solution)/shard_map/pallas_call | solution.py:305
  150.4 2.3 %copy.10 = f32[1,1,512,512]{3,2,1,0:T(8,128)} copy(f32[1,1,512,512]{3,2,1,0:T(8,128)} %get-tuple-element.4) | data formatting | bytes 2097152

commit v2 on v1

--- a/solution.py
+++ b/solution.py
@@ -17,9 +17,9 @@
     side, bonds, segs,
     ids, counts, env, site, right,
     out, corr,
-    e_all, a_all, w_acc, out_acc, right_in, term, terms_in,
+    e_all, a_all, w_acc, out_acc, parts, right_in, term, terms_in,
     ring_send, ring_recv, e_send, e_recv, a_send, a_recv,
-    right_send, right_recv, term_send, term_recv, local_sem,
+    right_send, right_recv, term_send, term_recv, local_sem, line_ready,
 ):
     chips = bonds // 2
     seg = lax.axis_index("seg")
@@ -37,37 +37,40 @@
     def mirrored(step):
         return (z + turn * step + 2 * chips) % chips
 
+    def turned(chip):
+        return (chip == chips // 4) | (chip == chips - 1 - chips // 4)
+
+    def crossed(chip):
+        return jnp.where(turned(chip) & (chip != z), 1, 0)
+
     def steps_from(chip, own_core):
         towards = jnp.where(own_core, z - chip, chip - z)
         return (towards * turn + 2 * chips) % chips
 
     following = (seg, ((z + turn + chips) % chips) * 2 + core)
-    previous = (seg, ((z - turn + chips) % chips) * 2 + core)
+    backward = (z - turn + chips) % chips
     sibling = (seg, z * 2 + 1 - core)
     has_before = seg > 0
     has_after = seg < segs - 1
 
     barrier = pltpu.get_barrier_semaphore()
-    pl.semaphore_signal(barrier, inc=1, device_id=previous, device_id_type=MESH)
+    for peer in range(2):
+        pl.semaphore_signal(barrier, inc=1, device_id=(seg, backward * 2 + peer), device_id_type=MESH)
     pl.semaphore_signal(barrier, inc=1, device_id=sibling, device_id_type=MESH)
 
     @pl.when(has_after)
     def _():
         pl.semaphore_signal(barrier, inc=1, device_id=(seg + 1, bond), device_id_type=MESH)
-
-    @pl.when(has_before)
-    def _():
-        for peer in range(bonds):
-            pl.semaphore_signal(barrier, inc=1, device_id=(seg - 1, peer), device_id_type=MESH)
 
     own_env = pltpu.make_async_copy(env.at[0, 0], e_all.at[bond], local_sem.at[0])
     own_site = pltpu.make_async_copy(site.at[0, 0], a_all.at[z], local_sem.at[1])
     own_env.start()
     own_site.start()
-    w_acc[...] = jnp.zeros_like(w_acc)
-    out_acc[...] = jnp.zeros_like(out_acc)
-
-    pl.semaphore_wait(barrier, 2 + jnp.where(has_before, 1, 0) + jnp.where(has_after, bonds, 0))
+    pl.semaphore_wait(barrier, 3 + jnp.where(has_before, 1, 0))
+
+    def site_following(step):
+        other = jnp.where(turned(z), step, 1) == 0
+        return (seg, jnp.where(other, backward * 2 + 1 - core, following[1]))
 
     def ring_copy(step, part):
         chip = chip_at(step)
@@ -78,7 +81,7 @@
         return pltpu.make_async_remote_copy(
             src_ref=ref, dst_ref=ref,
             send_sem=ring_send.at[step * 3 + part], recv_sem=ring_recv.at[step * 3 + part],
-            device_id=following, device_id_type=MESH,
+            device_id=following if part == 0 else site_following(step), device_id_type=MESH,
         )
 
     def ring_arrival(step, part):
@@ -100,22 +103,20 @@
             device_id=sibling, device_id_type=MESH,
         )
 
-    def site_across(chip):
+    def site_across(chip, from_core):
+        across_slot = jnp.where(column_of(chip, from_core) == row, chip // 2, side)
         return pltpu.make_async_remote_copy(
-            src_ref=a_all.at[chip], dst_ref=a_all.at[chips + chip // 2],
-            send_sem=a_send.at[chip // 2], recv_sem=a_recv.at[chip // 2],
+            src_ref=a_all.at[chip], dst_ref=a_all.at[chips + across_slot],
+            send_sem=a_send.at[across_slot], recv_sem=a_recv.at[across_slot],
             device_id=sibling, device_id_type=MESH,
         )
 
     def column_of(chip, at_core):
-        return 2 * (chip % 2) + at_core
-
-    def site_goes_on(step):
-        target = (z + turn + chips) % chips
-        return (step < chips - 2) | ((step == chips - 2) & (target // 2 == column_of(chip_at(step), core)))
-
-    def site_comes(step):
-        return (step < chips - 1) | ((step == chips - 1) & (row == column_of(chip_at(step), core)))
+        return 2 * (chip % 2) + (at_core + crossed(chip)) % 2
+
+    def needed_across(chip, from_core):
+        found = column_of(chip, from_core)
+        return (found == row) | (found == 2 * half + 1 - from_core)
 
     own_env.wait()
     ring_copy(0, 0).start()
@@ -124,9 +125,9 @@
     ring_copy(0, 2).start()
     env_across(0, z, core).start()
 
-    @pl.when(column_of(z, core) == row)
-    def _():
-        site_across(z).start()
+    @pl.when(needed_across(z, core))
+    def _():
+        site_across(z, core).start()
 
     @pl.when(has_before)
     def _():
@@ -134,6 +135,9 @@
             src_ref=right.at[0, 0], dst_ref=right_in, send_sem=right_send, recv_sem=right_recv,
             device_id=(seg - 1, bond), device_id_type=MESH,
         ).start()
+
+    w_acc[...] = jnp.zeros_like(w_acc)
+    out_acc[...] = jnp.zeros_like(out_acc)
 
     tally = [jnp.float32(0.0)] * 3
     for k in range(ids.shape[1]):
@@ -142,25 +146,40 @@
     half_z = 0.5 * tally[0]
     operator = ((half_z, 0.5 * tally[1] + 0.5 * tally[2]), (0.5 * tally[1] - 0.5 * tally[2], -half_z))
 
+    def taken_up(chip, at_core):
+        mine = at_core == core
+        return 2 * steps_from(chip, mine) + jnp.where(mine, 0, 1)
+
     def env_step(a, k):
-        return steps_from(2 * a + k // 2, k % 2 == core)
+        return taken_up(2 * a + k // 2, k % 2)
 
     def site_step(k):
-        return steps_from(2 * k + half, jnp.bool_(True))
+        chip = 2 * k + half
+        return taken_up(chip, (core + crossed(chip)) % 2)
+
+    def site_slot(k):
+        chip = 2 * k + half
+        return jnp.where(crossed(chip) == 0, chip, chips + jnp.where(column == row, k, side))
 
     def left_step(a):
-        return steps_from(2 * a + row // 2, row % 2 == core)
-
-    def compute(step):
+        chip = 2 * a + row // 2
+        return taken_up(chip, (row + crossed(chip)) % 2)
+
+    def left_slot(a):
+        chip = 2 * a + row // 2
+        return jnp.where((row + crossed(chip)) % 2 == core, chip, chips + a)
+
+    def compute(phase):
         def first(i, carry):
             a = i // side
             k = i % side
 
-            @pl.when(jnp.maximum(env_step(a, k), site_step(k)) == step)
+            @pl.when(jnp.maximum(env_step(a, k), site_step(k)) == phase)
             def _():
                 block = e_all[a * side + k]
+                slot = site_slot(k)
                 for t in range(2):
-                    w_acc[a, t] += jnp.dot(block, a_all[2 * k + half, t], preferred_element_type=F32)
+                    w_acc[a, t] += jnp.dot(block, a_all[slot, t], preferred_element_type=F32)
 
             return carry
 
@@ -171,17 +190,18 @@
             for k in range(side):
                 latest = jnp.maximum(latest, jnp.maximum(env_step(a, k), site_step(k)))
 
-            @pl.when(latest == step)
+            @pl.when(latest == phase)
             def _():
-                slot = jnp.where(row % 2 == core, 2 * a + row // 2, chips + a)
+                slot = left_slot(a)
+                size = out_acc.shape[0]
                 for s in range(2):
                     weighted = operator[s][0] * w_acc[a, 0] + operator[s][1] * w_acc[a, 1]
                     high = weighted.astype(BF16)
-                    low = (weighted - high.astype(F32)).astype(BF16)
-                    left = a_all[slot, s]
+                    parts[:, :size] = high
+                    parts[:, size:] = (weighted - high.astype(F32)).astype(BF16)
                     dims = (((0,), (0,)), ((), ()))
-                    out_acc[...] += lax.dot_general(left, high, dims, preferred_element_type=F32)
-                    out_acc[...] += lax.dot_general(left, low, dims, preferred_element_type=F32)
+                    both = lax.dot_general(a_all[slot, s], parts[...], dims, preferred_element_type=F32)
+                    out_acc[...] += both[:, :size] + both[:, size:]
 
             return carry
 
@@ -191,14 +211,20 @@
         chip = mirrored(step)
         env_across(step, chip, 1 - core).wait_recv()
 
-        @pl.when((row % 2 != core) & (column_of(chip, 1 - core) == row))
-        def _():
-            site_across(chip).wait_recv()
-
-    across_arrivals(0)
+        @pl.when((step < chips - 1) & needed_across(chip, 1 - core))
+        def _():
+            site_across(chip, 1 - core).wait_recv()
+
     compute(0)
 
     def turn_of(step, carry):
+        across_arrivals(step - 1)
+
+        @pl.when((step == chips // 2 + 1) & has_before)
+        def _():
+            pl.semaphore_signal(line_ready, inc=1, device_id=(seg - 1, bond), device_id_type=MESH)
+
+        compute(2 * step - 1)
         ring_arrival(step, 0).wait_recv()
 
         @pl.when(step < chips - 1)
@@ -207,24 +233,25 @@
 
         env_across(step, chip_at(step), core).start()
 
-        @pl.when(site_comes(step))
+        @pl.when(step < chips - 1)
         def _():
             for part in (1, 2):
                 ring_arrival(step, part).wait_recv()
 
-                @pl.when(site_goes_on(step))
+                @pl.when(step < chips - 2)
                 def _():
                     ring_copy(step, part).start()
 
-            @pl.when(column_of(chip_at(step), core) == row)
+            @pl.when(needed_across(chip_at(step), core))
             def _():
-                site_across(chip_at(step)).start()
-
-        across_arrivals(step)
-        compute(step)
+                site_across(chip_at(step), core).start()
+
+        compute(2 * step)
         return carry
 
     lax.fori_loop(1, chips, turn_of, 0)
+    across_arrivals(chips - 1)
+    compute(2 * chips - 1)
 
     store = pltpu.make_async_copy(out_acc, out.at[0, 0], local_sem.at[2])
     store.start()
@@ -242,6 +269,7 @@
         for at in range(128, size, 128):
             total = total + folded[:, at : at + 128]
         term[...] = total
+        pl.semaphore_wait(line_ready, 1)
         for peer in range(bonds):
             pltpu.make_async_remote_copy(
                 src_ref=term, dst_ref=terms_in.at[bond], send_sem=term_send.at[peer], recv_sem=term_recv,
@@ -276,16 +304,16 @@
         def _():
             ring_copy(step, 0).wait_send()
 
-            @pl.when(site_goes_on(step))
-            def _():
-                ring_copy(step, 1).wait_send()
-                ring_copy(step, 2).wait_send()
+        @pl.when(step < chips - 2)
+        def _():
+            ring_copy(step, 1).wait_send()
+            ring_copy(step, 2).wait_send()
 
         env_across(step, chip_at(step), core).wait_send()
 
-        @pl.when(column_of(chip_at(step), core) == row)
-        def _():
-            site_across(chip_at(step)).wait_send()
+        @pl.when((step < chips - 1) & needed_across(chip_at(step), core))
+        def _():
+            site_across(chip_at(step), core).wait_send()
 
         return carry
 
@@ -312,9 +340,10 @@
         out_specs=(hbm, smem),
         scratch_shapes=[
             pltpu.VMEM((bonds, size, size), BF16),
-            pltpu.VMEM((chips + side, 2, size, size), BF16),
+            pltpu.VMEM((chips + side + 1, 2, size, size), BF16),
             pltpu.VMEM((side, 2, size, size), F32),
             pltpu.VMEM((size, size), F32),
+            pltpu.VMEM((size, 2 * size), BF16),
             pltpu.VMEM((size, size), BF16),
             pltpu.VMEM((8, 128), F32),
             pltpu.VMEM((bonds, 8, 128), F32),
@@ -322,13 +351,14 @@
             dma((3 * (chips - 1),)),
             dma((chips,)),
             dma((chips,)),
-            dma((side,)),
-            dma((side,)),
+            dma((side + 1,)),
+            dma((side + 1,)),
             dma,
             dma,
             dma((bonds,)),
             dma,
             dma((3,)),
+            pltpu.SemaphoreType.REGULAR,
         ],
         compiler_params=pltpu.CompilerParams(
             collective_id=0, has_side_effects=True, vmem_limit_bytes=56 * 2**20

time: 155 us -> 145 us (0.935)
  Pallas kernels: 149 us -> 139 us
    pallas_call x1, Pallas kernels: 149 us -> 139 us  [body(): pl.pallas_call(functools.partial(kernel, side, bonds, segs), out_shape=(j...]
where the time goes in v2:
time: 145 us
  Pallas kernels  139 us (96%)
  between operations  2.97 us (2%)
  local copies, waits for them, and re-layouts  2.26 us (2%)
    pallas_call x1, Pallas kernels, body(): pl.pallas_call(functools.partial(kernel, side, bonds, segs), out_shape=(j...  139 us

profile of v2, /device:TPU:7, one launch (start us, length us, event | category | flops | bytes accessed | tf_op | source)
XLA Modules:
  0.0 144.5 jit_solution(4259445002109079724)
XLA Ops:
  1.3 139.3 %shard_map.68 = (f32[1,1,512,512]{3,2,1,0:T(8,128)}, f32[1]{0:T(128)}) custom-call(s32[1,4]{1,0:T(1,128)} %ids.1, s32[1]{0:T(128)S(6)} %copy.9.counts, bf16[1,1,512,512]{3,2,1,0:T(8,128)(2,1)} %env.1, bf16[1,1,2,512,512]{4,3,2,1,0:T(8,128)(2,1)} %site.1, bf16[1,1,512,512]{3,2,1,0:T(8,128)(2,1)} %right.1), custom_call_target="tpu_custom_call" | custom-call | flops 25999998976 | bytes 6291456 | tf_op jit(solution)/shard_map/pallas_call | solution.py:333
  140.6 2.3 %copy.10 = f32[1,1,512,512]{3,2,1,0:T(8,128)} copy(f32[1,1,512,512]{3,2,1,0:T(8,128)} %get-tuple-element.4) | data formatting | bytes 2097152

commit v3 on v2

--- a/solution.py
+++ b/solution.py
@@ -22,6 +22,8 @@
     right_send, right_recv, term_send, term_recv, local_sem, line_ready,
 ):
     chips = bonds // 2
+    size = out_acc.shape[0]
+    rows = size // 2
     seg = lax.axis_index("seg")
     bond = lax.axis_index("bond")
     z = bond // 2
@@ -72,42 +74,41 @@
         other = jnp.where(turned(z), step, 1) == 0
         return (seg, jnp.where(other, backward * 2 + 1 - core, following[1]))
 
+    def ring_ref(step, part):
+        chip = chip_at(step)
+        if isinstance(part, int) and part >= 2:
+            return a_all.at[chip, part - 2]
+        return e_all.at[chip * 2 + core, pl.ds(part * rows, rows)]
+
     def ring_copy(step, part):
-        chip = chip_at(step)
-        if part == 0:
-            ref = e_all.at[chip * 2 + core]
-        else:
-            ref = a_all.at[chip, part - 1]
+        ref = ring_ref(step, part)
+        site_part = isinstance(part, int) and part >= 2
         return pltpu.make_async_remote_copy(
             src_ref=ref, dst_ref=ref,
-            send_sem=ring_send.at[step * 3 + part], recv_sem=ring_recv.at[step * 3 + part],
-            device_id=following if part == 0 else site_following(step), device_id_type=MESH,
+            send_sem=ring_send.at[step * 4 + part], recv_sem=ring_recv.at[step * 4 + part],
+            device_id=site_following(step) if site_part else following, device_id_type=MESH,
         )
 
     def ring_arrival(step, part):
-        chip = chip_at(step)
-        if part == 0:
-            ref = e_all.at[chip * 2 + core]
-        else:
-            ref = a_all.at[chip, part - 1]
+        ref = ring_ref(step, part)
         return pltpu.make_async_remote_copy(
             src_ref=ref, dst_ref=ref,
-            send_sem=ring_send.at[(step - 1) * 3 + part], recv_sem=ring_recv.at[(step - 1) * 3 + part],
+            send_sem=ring_send.at[step * 4 - 4 + part], recv_sem=ring_recv.at[step * 4 - 4 + part],
             device_id=following, device_id_type=MESH,
         )
 
-    def env_across(step, chip, at_core):
-        ref = e_all.at[chip * 2 + at_core]
+    def env_across(step, part, chip, at_core):
+        ref = e_all.at[chip * 2 + at_core, pl.ds(part * rows, rows)]
         return pltpu.make_async_remote_copy(
-            src_ref=ref, dst_ref=ref, send_sem=e_send.at[step], recv_sem=e_recv.at[step],
+            src_ref=ref, dst_ref=ref, send_sem=e_send.at[step * 2 + part], recv_sem=e_recv.at[step * 2 + part],
             device_id=sibling, device_id_type=MESH,
         )
 
-    def site_across(chip, from_core):
+    def site_across(chip, from_core, state):
         across_slot = jnp.where(column_of(chip, from_core) == row, chip // 2, side)
         return pltpu.make_async_remote_copy(
-            src_ref=a_all.at[chip], dst_ref=a_all.at[chips + across_slot],
-            send_sem=a_send.at[across_slot], recv_sem=a_recv.at[across_slot],
+            src_ref=a_all.at[chip, state], dst_ref=a_all.at[chips + across_slot, state],
+            send_sem=a_send.at[2 * across_slot + state], recv_sem=a_recv.at[2 * across_slot + state],
             device_id=sibling, device_id_type=MESH,
         )
 
@@ -118,16 +119,19 @@
         found = column_of(chip, from_core)
         return (found == row) | (found == 2 * half + 1 - from_core)
 
+    own_site.wait()
+    ring_copy(0, 2).start()
+    ring_copy(0, 3).start()
     own_env.wait()
     ring_copy(0, 0).start()
-    own_site.wait()
     ring_copy(0, 1).start()
-    ring_copy(0, 2).start()
-    env_across(0, z, core).start()
+    env_across(0, 0, z, core).start()
+    env_across(0, 1, z, core).start()
 
     @pl.when(needed_across(z, core))
     def _():
-        site_across(z, core).start()
+        for state in range(2):
+            site_across(z, core, state).start()
 
     @pl.when(has_before)
     def _():
@@ -146,112 +150,182 @@
     half_z = 0.5 * tally[0]
     operator = ((half_z, 0.5 * tally[1] + 0.5 * tally[2]), (0.5 * tally[1] - 0.5 * tally[2], -half_z))
 
-    def taken_up(chip, at_core):
+    def env_phase(a, k):
+        mine = k % 2 == core
+        return 6 * steps_from(2 * a + k // 2, mine) + jnp.where(mine, 2, 4)
+
+    def site_phase(chip, at_core):
         mine = at_core == core
-        return 2 * steps_from(chip, mine) + jnp.where(mine, 0, 1)
-
-    def env_step(a, k):
-        return taken_up(2 * a + k // 2, k % 2)
-
-    def site_step(k):
+        return 6 * steps_from(chip, mine) + jnp.where(mine, 0, 1)
+
+    def column_phase(k):
         chip = 2 * k + half
-        return taken_up(chip, (core + crossed(chip)) % 2)
-
-    def site_slot(k):
+        return site_phase(chip, (core + crossed(chip)) % 2)
+
+    def column_slot(k):
         chip = 2 * k + half
         return jnp.where(crossed(chip) == 0, chip, chips + jnp.where(column == row, k, side))
 
-    def left_step(a):
+    def left_phase(a):
         chip = 2 * a + row // 2
-        return taken_up(chip, (row + crossed(chip)) % 2)
+        return site_phase(chip, (row + crossed(chip)) % 2)
 
     def left_slot(a):
         chip = 2 * a + row // 2
         return jnp.where((row + crossed(chip)) % 2 == core, chip, chips + a)
 
-    def compute(phase):
-        def first(i, carry):
-            a = i // side
-            k = i % side
-
-            @pl.when(jnp.maximum(env_step(a, k), site_step(k)) == phase)
+    all_columns = jnp.int32(0)
+    for k in range(side):
+        all_columns = jnp.maximum(all_columns, column_phase(k))
+    last_env = []
+    last_site = []
+    for a in range(side):
+        latest = env_phase(a, 0)
+        for k in range(1, side):
+            latest = jnp.maximum(latest, env_phase(a, k))
+        last_env.append(latest)
+        last_site.append(jnp.maximum(all_columns, left_phase(a)))
+
+    def picked(values, a):
+        found = values[side - 1]
+        for at in range(side - 1):
+            found = jnp.where(a == at, values[at], found)
+        return found
+
+    def add_product(a, k, part, states):
+        block = e_all[a * side + k, pl.ds(part * rows, rows)]
+        slot = column_slot(k)
+        for t in states:
+            w_acc[a, t, pl.ds(part * rows, rows)] += jnp.dot(block, a_all[slot, t], preferred_element_type=F32)
+
+    def finish(a, part, phase):
+        @pl.when(jnp.maximum(picked(last_env, a) + part, picked(last_site, a)) == phase)
+        def _():
+            here = pl.ds(part * rows, rows)
+            for s in range(2):
+                weighted = operator[s][0] * w_acc[a, 0, here] + operator[s][1] * w_acc[a, 1, here]
+                high = weighted.astype(BF16)
+                parts[s * rows : (s + 1) * rows, :size] = high
+                parts[s * rows : (s + 1) * rows, size:] = (weighted - high.astype(F32)).astype(BF16)
+            left = a_all[left_slot(a), :, here].reshape(size, size)
+            both = lax.dot_general(left, parts[...], (((0,), (0,)), ((), ())), preferred_element_type=F32)
+            out_acc[...] += both[:, :size] + both[:, size:]
+
+    def take_env(chip, at_core, part, phase):
+        a = chip // 2
+        k = 2 * (chip % 2) + at_core
+
+        @pl.when(column_phase(k) < phase)
+        def _():
+            add_product(a, k, part, (0, 1))
+
+        finish(a, part, phase)
+
+    def take_site(chip, at_core, phase, state):
+        k = chip // 2
+
+        def one(i, carry):
+            a = i // 2
+            part = i % 2
+
+            @pl.when(env_phase(a, k) + part < phase)
             def _():
-                block = e_all[a * side + k]
-                slot = site_slot(k)
-                for t in range(2):
-                    w_acc[a, t] += jnp.dot(block, a_all[slot, t], preferred_element_type=F32)
+                add_product(a, k, part, (state,))
 
             return carry
 
-        lax.fori_loop(0, side * side, first, 0)
-
-        def second(a, carry):
-            latest = left_step(a)
-            for k in range(side):
-                latest = jnp.maximum(latest, jnp.maximum(env_step(a, k), site_step(k)))
-
-            @pl.when(latest == phase)
+        @pl.when(column_of(chip, at_core) == column)
+        def _():
+            lax.fori_loop(0, 2 * side, one, 0)
+
+    def finish_site(chip, at_core, phase):
+        found = column_of(chip, at_core)
+
+        def one(i, carry):
+            finish(i // 2, i % 2, phase)
+            return carry
+
+        @pl.when((found == column) | (found == row))
+        def _():
+            lax.fori_loop(0, 2 * side, one, 0)
+
+    def own_halves(step):
+        def one(part, carry):
+            @pl.when(step > 0)
             def _():
-                slot = left_slot(a)
-                size = out_acc.shape[0]
-                for s in range(2):
-                    weighted = operator[s][0] * w_acc[a, 0] + operator[s][1] * w_acc[a, 1]
-                    high = weighted.astype(BF16)
-                    parts[:, :size] = high
-                    parts[:, size:] = (weighted - high.astype(F32)).astype(BF16)
-                    dims = (((0,), (0,)), ((), ()))
-                    both = lax.dot_general(a_all[slot, s], parts[...], dims, preferred_element_type=F32)
-                    out_acc[...] += both[:, :size] + both[:, size:]
-
+                ring_arrival(step, part).wait_recv()
+
+                @pl.when(step < chips - 1)
+                def _():
+                    ring_copy(step, part).start()
+
+                env_across(step, part, chip_at(step), core).start()
+
+            take_env(chip_at(step), core, part, 6 * step + 2 + part)
             return carry
 
-        lax.fori_loop(0, side, second, 0)
-
-    def across_arrivals(step):
+        lax.fori_loop(0, 2, one, 0)
+
+    def across_halves(step):
         chip = mirrored(step)
-        env_across(step, chip, 1 - core).wait_recv()
-
-        @pl.when((step < chips - 1) & needed_across(chip, 1 - core))
-        def _():
-            site_across(chip, 1 - core).wait_recv()
-
-    compute(0)
-
-    def turn_of(step, carry):
-        across_arrivals(step - 1)
-
-        @pl.when((step == chips // 2 + 1) & has_before)
-        def _():
-            pl.semaphore_signal(line_ready, inc=1, device_id=(seg - 1, bond), device_id_type=MESH)
-
-        compute(2 * step - 1)
-        ring_arrival(step, 0).wait_recv()
-
-        @pl.when(step < chips - 1)
-        def _():
-            ring_copy(step, 0).start()
-
-        env_across(step, chip_at(step), core).start()
-
-        @pl.when(step < chips - 1)
-        def _():
-            for part in (1, 2):
-                ring_arrival(step, part).wait_recv()
+
+        def one(part, carry):
+            env_across(step, part, chip, 1 - core).wait_recv()
+            take_env(chip, 1 - core, part, 6 * step + 4 + part)
+            return carry
+
+        lax.fori_loop(0, 2, one, 0)
+
+    def own_site(step):
+        chip = chip_at(step)
+        for state in range(2):
+            @pl.when(step > 0)
+            def _():
+                ring_arrival(step, 2 + state).wait_recv()
 
                 @pl.when(step < chips - 2)
                 def _():
-                    ring_copy(step, part).start()
-
-            @pl.when(needed_across(chip_at(step), core))
+                    ring_copy(step, 2 + state).start()
+
+                @pl.when(needed_across(chip, core))
+                def _():
+                    site_across(chip, core, state).start()
+
+            take_site(chip, core, 6 * step, state)
+
+    def sibling_site(step):
+        chip = mirrored(step)
+
+        @pl.when(needed_across(chip, 1 - core))
+        def _():
+            for state in range(2):
+                site_across(chip, 1 - core, state).wait_recv()
+                take_site(chip, 1 - core, 6 * step + 1, state)
+
+    def turn_of(step, carry):
+        @pl.when(step < chips - 1)
+        def _():
+            own_site(step)
+            sibling_site(step)
+
+        own_halves(step)
+
+        @pl.when(step < chips - 1)
+        def _():
+            finish_site(chip_at(step), core, 6 * step)
+
+            @pl.when(needed_across(mirrored(step), 1 - core))
             def _():
-                site_across(chip_at(step), core).start()
-
-        compute(2 * step)
+                finish_site(mirrored(step), 1 - core, 6 * step + 1)
+
+        @pl.when((step == chips // 2 + 1) & has_before)
+        def _():
+            pl.semaphore_signal(line_ready, inc=1, device_id=(seg - 1, bond), device_id_type=MESH)
+
+        across_halves(step)
         return carry
 
-    lax.fori_loop(1, chips, turn_of, 0)
-    across_arrivals(chips - 1)
-    compute(2 * chips - 1)
+    lax.fori_loop(0, chips, turn_of, 0)
 
     store = pltpu.make_async_copy(out_acc, out.at[0, 0], local_sem.at[2])
     store.start()
@@ -262,7 +336,6 @@
             src_ref=right.at[0, 0], dst_ref=right_in, send_sem=right_send, recv_sem=right_recv,
             device_id=(seg, bond), device_id_type=MESH,
         ).wait_recv()
-        size = out_acc.shape[0]
         products = out_acc[...] * right_in[...].astype(F32)
         folded = jnp.sum(products.reshape(size // 8, 8, size), axis=0)
         total = folded[:, :128]
@@ -284,8 +357,7 @@
             src_ref=terms_in, dst_ref=terms_in, send_sem=term_send.at[0], recv_sem=term_recv,
             device_id=(seg, bond), device_id_type=MESH,
         ).wait_recv()
-        size = out_acc.shape[0] * side
-        corr[0] = jnp.sum(terms_in[...]) * (1.0 / size)
+        corr[0] = jnp.sum(terms_in[...]) * (1.0 / (size * side))
         pltpu.make_async_remote_copy(
             src_ref=right.at[0, 0], dst_ref=right_in, send_sem=right_send, recv_sem=right_recv,
             device_id=(seg, bond), device_id_type=MESH,
@@ -303,17 +375,20 @@
         @pl.when(step < chips - 1)
         def _():
             ring_copy(step, 0).wait_send()
+            ring_copy(step, 1).wait_send()
 
         @pl.when(step < chips - 2)
         def _():
-            ring_copy(step, 1).wait_send()
             ring_copy(step, 2).wait_send()
-
-        env_across(step, chip_at(step), core).wait_send()
+            ring_copy(step, 3).wait_send()
+
+        env_across(step, 0, chip_at(step), core).wait_send()
+        env_across(step, 1, chip_at(step), core).wait_send()
 
         @pl.when((step < chips - 1) & needed_across(chip_at(step), core))
         def _():
-            site_across(chip_at(step), core).wait_send()
+            for state in range(2):
+                site_across(chip_at(step), core, state).wait_send()
 
         return carry
 
@@ -347,12 +422,12 @@
             pltpu.VMEM((size, size), BF16),
             pltpu.VMEM((8, 128), F32),
             pltpu.VMEM((bonds, 8, 128), F32),
-            dma((3 * (chips - 1),)),
-            dma((3 * (chips - 1),)),
-            dma((chips,)),
-            dma((chips,)),
-            dma((side + 1,)),
-            dma((side + 1,)),
+            dma((4 * (chips - 1),)),
+            dma((4 * (chips - 1),)),
+            dma((2 * chips,)),
+            dma((2 * chips,)),
+            dma((2 * side + 2,)),
+            dma((2 * side + 2,)),
             dma,
             dma,
             dma((bonds,)),

time: 145 us -> 141 us (0.972)
  Pallas kernels: 139 us -> 136 us
    pallas_call x1, Pallas kernels: 139 us -> 136 us  [body(): pl.pallas_call(functools.partial(kernel, side, bonds, segs), out_shape=(j...]
where the time goes in v3:
time: 141 us
  Pallas kernels  136 us (96%)
  between operations  2.97 us (2%)
  local copies, waits for them, and re-layouts  2.26 us (2%)
    pallas_call x1, Pallas kernels, body(): pl.pallas_call(functools.partial(kernel, side, bonds, segs), out_shape=(j...  136 us

profile of v3, /device:TPU:7, one launch (start us, length us, event | category | flops | bytes accessed | tf_op | source)
XLA Modules:
  0.0 140.9 jit_solution(14248543103257767353)
XLA Ops:
  1.3 135.6 %shard_map.68 = (f32[1,1,512,512]{3,2,1,0:T(8,128)}, f32[1]{0:T(128)}) custom-call(s32[1,4]{1,0:T(1,128)} %ids.1, s32[1]{0:T(128)S(6)} %copy.9.counts, bf16[1,1,512,512]{3,2,1,0:T(8,128)(2,1)} %env.1, bf16[1,1,2,512,512]{4,3,2,1,0:T(8,128)(2,1)} %site.1, bf16[1,1,512,512]{3,2,1,0:T(8,128)(2,1)} %right.1), custom_call_target="tpu_custom_call" | custom-call | flops 25999998976 | bytes 6291456 | tf_op jit(solution)/shard_map/pallas_call | solution.py:408
  136.9 2.3 %copy.10 = f32[1,1,512,512]{3,2,1,0:T(8,128)} copy(f32[1,1,512,512]{3,2,1,0:T(8,128)} %get-tuple-element.4) | data formatting | bytes 2097152

commit v4 on v3

--- a/solution.py
+++ b/solution.py
@@ -17,11 +17,12 @@
     side, bonds, segs,
     ids, counts, env, site, right,
     out, corr,
-    e_all, a_all, w_acc, out_acc, parts, right_in, term, terms_in,
+    e_all, a_all, w_acc, parts, right_in, term, terms_in,
     ring_send, ring_recv, e_send, e_recv, a_send, a_recv,
     right_send, right_recv, term_send, term_recv, local_sem, line_ready,
 ):
     chips = bonds // 2
+    out_acc = out.at[0, 0]
     size = out_acc.shape[0]
     rows = size // 2
     seg = lax.axis_index("seg")
@@ -147,8 +148,7 @@
     for k in range(ids.shape[1]):
         for c in range(3):
             tally[c] = tally[c] + jnp.where((k < counts[0]) & (ids[0, k] == c), jnp.float32(1.0), jnp.float32(0.0))
-    half_z = 0.5 * tally[0]
-    operator = ((half_z, 0.5 * tally[1] + 0.5 * tally[2]), (0.5 * tally[1] - 0.5 * tally[2], -half_z))
+    doubled = ((tally[0], tally[1] + tally[2]), (tally[1] - tally[2], -tally[0]))
 
     def env_phase(a, k):
         mine = k % 2 == core
@@ -203,7 +203,7 @@
         def _():
             here = pl.ds(part * rows, rows)
             for s in range(2):
-                weighted = operator[s][0] * w_acc[a, 0, here] + operator[s][1] * w_acc[a, 1, here]
+                weighted = doubled[s][0] * w_acc[a, 0, here] + doubled[s][1] * w_acc[a, 1, here]
                 high = weighted.astype(BF16)
                 parts[s * rows : (s + 1) * rows, :size] = high
                 parts[s * rows : (s + 1) * rows, size:] = (weighted - high.astype(F32)).astype(BF16)
@@ -249,18 +249,15 @@
         def _():
             lax.fori_loop(0, 2 * side, one, 0)
 
+    def env_comes(step, part):
+        @pl.when(step > 0)
+        def _():
+            ring_arrival(step, part).wait_recv()
+            ring_copy(step, part).start()
+            env_across(step, part, chip_at(step), core).start()
+
     def own_halves(step):
         def one(part, carry):
-            @pl.when(step > 0)
-            def _():
-                ring_arrival(step, part).wait_recv()
-
-                @pl.when(step < chips - 1)
-                def _():
-                    ring_copy(step, part).start()
-
-                env_across(step, part, chip_at(step), core).start()
-
             take_env(chip_at(step), core, part, 6 * step + 2 + part)
             return carry
 
@@ -276,47 +273,50 @@
 
         lax.fori_loop(0, 2, one, 0)
 
-    def own_site(step):
+    def own_site(step, state):
         chip = chip_at(step)
-        for state in range(2):
-            @pl.when(step > 0)
+
+        @pl.when(step > 0)
+        def _():
+            ring_arrival(step, 2 + state).wait_recv()
+
+            @pl.when(step < chips - 2)
             def _():
-                ring_arrival(step, 2 + state).wait_recv()
-
-                @pl.when(step < chips - 2)
-                def _():
-                    ring_copy(step, 2 + state).start()
-
-                @pl.when(needed_across(chip, core))
-                def _():
-                    site_across(chip, core, state).start()
-
-            take_site(chip, core, 6 * step, state)
-
-    def sibling_site(step):
+                ring_copy(step, 2 + state).start()
+
+            @pl.when(needed_across(chip, core))
+            def _():
+                site_across(chip, core, state).start()
+
+        take_site(chip, core, 6 * step, state)
+
+    def sibling_site(step, state):
         chip = mirrored(step)
 
+        @pl.when(column_of(chip, 1 - core) == column)
+        def _():
+            site_across(chip, 1 - core, state).wait_recv()
+            take_site(chip, 1 - core, 6 * step + 1, state)
+
+    def turn_of(step, carry):
+        own_site(step, 0)
+        sibling_site(step, 0)
+        own_site(step, 1)
+        env_comes(step, 0)
+        sibling_site(step, 1)
+        env_comes(step, 1)
+        own_halves(step)
+        finish_site(chip_at(step), core, 6 * step)
+        chip = mirrored(step)
+
         @pl.when(needed_across(chip, 1 - core))
         def _():
-            for state in range(2):
-                site_across(chip, 1 - core, state).wait_recv()
-                take_site(chip, 1 - core, 6 * step + 1, state)
-
-    def turn_of(step, carry):
-        @pl.when(step < chips - 1)
-        def _():
-            own_site(step)
-            sibling_site(step)
-
-        own_halves(step)
-
-        @pl.when(step < chips - 1)
-        def _():
-            finish_site(chip_at(step), core, 6 * step)
-
-            @pl.when(needed_across(mirrored(step), 1 - core))
+            @pl.when(column_of(chip, 1 - core) != column)
             def _():
-                finish_site(mirrored(step), 1 - core, 6 * step + 1)
+                for state in range(2):
+                    site_across(chip, 1 - core, state).wait_recv()
+
+            finish_site(chip, 1 - core, 6 * step + 1)
 
         @pl.when((step == chips // 2 + 1) & has_before)
         def _():
@@ -325,10 +325,18 @@
         across_halves(step)
         return carry
 
-    lax.fori_loop(0, chips, turn_of, 0)
-
-    store = pltpu.make_async_copy(out_acc, out.at[0, 0], local_sem.at[2])
-    store.start()
+    lax.fori_loop(0, chips - 1, turn_of, 0)
+
+    def last_turn(part, carry):
+        step = chips - 1
+        ring_arrival(step, part).wait_recv()
+        env_across(step, part, chip_at(step), core).start()
+        take_env(chip_at(step), core, part, 6 * step + 2 + part)
+        env_across(step, part, mirrored(step), 1 - core).wait_recv()
+        take_env(mirrored(step), 1 - core, part, 6 * step + 4 + part)
+        return carry
+
+    lax.fori_loop(0, 2, last_turn, 0)
 
     @pl.when(has_after)
     def _():
@@ -357,7 +365,7 @@
             src_ref=terms_in, dst_ref=terms_in, send_sem=term_send.at[0], recv_sem=term_recv,
             device_id=(seg, bond), device_id_type=MESH,
         ).wait_recv()
-        corr[0] = jnp.sum(terms_in[...]) * (1.0 / (size * side))
+        corr[0] = jnp.sum(terms_in[...]) * (0.5 / (size * side))
         pltpu.make_async_remote_copy(
             src_ref=right.at[0, 0], dst_ref=right_in, send_sem=right_send, recv_sem=right_recv,
             device_id=(seg, bond), device_id_type=MESH,
@@ -393,7 +401,6 @@
         return carry
 
     lax.fori_loop(0, chips, drain, 0)
-    store.wait()
 
 
 def body(env_in, site, right_env, comp_ids, counts):
@@ -402,22 +409,21 @@
     side = math.isqrt(bonds)
     chips = bonds // 2
     size = env_in.shape[-1]
-    hbm = pl.BlockSpec(memory_space=pl.ANY)
+    hbm = pl.BlockSpec(memory_space=pltpu.HBM)
     smem = pl.BlockSpec(memory_space=pltpu.SMEM)
     dma = pltpu.SemaphoreType.DMA
-    return pl.pallas_call(
+    twice, closed = pl.pallas_call(
         functools.partial(kernel, side, bonds, segs),
         out_shape=(
-            jax.ShapeDtypeStruct((1, 1, size, size), F32),
+            pltpu.VMEM((1, 1, size, size), F32),
             jax.ShapeDtypeStruct((1,), F32),
         ),
         in_specs=[smem, smem, hbm, hbm, hbm],
-        out_specs=(hbm, smem),
+        out_specs=(pl.BlockSpec(memory_space=pltpu.VMEM), smem),
         scratch_shapes=[
             pltpu.VMEM((bonds, size, size), BF16),
             pltpu.VMEM((chips + side + 1, 2, size, size), BF16),
             pltpu.VMEM((side, 2, size, size), F32),
-            pltpu.VMEM((size, size), F32),
             pltpu.VMEM((size, 2 * size), BF16),
             pltpu.VMEM((size, size), BF16),
             pltpu.VMEM((8, 128), F32),
@@ -432,7 +438,7 @@
             dma,
             dma((bonds,)),
             dma,
-            dma((3,)),
+            dma((2,)),
             pltpu.SemaphoreType.REGULAR,
         ],
         compiler_params=pltpu.CompilerParams(
@@ -440,6 +446,7 @@
         ),
         cost_estimate=pl.CostEstimate(flops=26 * 10**9, bytes_accessed=6 * 2**20, transcendentals=0),
     )(comp_ids, counts, env_in, site, right_env)
+    return twice * 0.5, closed
 
 
 def solution(mesh):

time: 141 us -> 139 us (0.986)
  local copies, waits for them, and re-layouts: 2.26 us -> 0 us
    unnamed x1 -> x0, local copies, waits for them, and re-layouts: 2.26 us -> none
where the time goes in v4:
time: 139 us
  Pallas kernels  135 us (97%)
  between operations  2.97 us (2%)
    pallas_call x1, Pallas kernels, body(): pl.pallas_call(functools.partial(kernel, side, bonds, segs), out_shape=(p...  135 us

profile of v4, /device:TPU:7, one launch (start us, length us, event | category | flops | bytes accessed | tf_op | source)
XLA Modules:
  0.0 138.7 jit_solution(14792653561022633285)
XLA Ops:
  1.3 134.7 %shard_map.68 = (f32[1,1,512,512]{3,2,1,0:T(8,128)S(1)}, f32[1]{0:T(128)}) custom-call(s32[1,4]{1,0:T(1,128)} %ids.1, s32[1]{0:T(128)S(6)} %copy.8.counts, bf16[1,1,512,512]{3,2,1,0:T(8,128)(2,1)} %env.1, bf16[1,1,2,512,512]{4,3,2,1,0:T(8,128)(2,1)} %site.1, bf16[1,1,512,512]{3,2,1,0:T(8,128)(2,1)} %right.1), custom_call_target="tpu_custom_call" | custom-call | flops 25999998976 | bytes 6291456 | tf_op jit(solution)/shard_map/pallas_call | solution.py:415
  136.0 1.1 broadcast_multiply_fusion

commit v5 on v4

--- a/solution.py
+++ b/solution.py
@@ -205,11 +205,11 @@
             for s in range(2):
                 weighted = doubled[s][0] * w_acc[a, 0, here] + doubled[s][1] * w_acc[a, 1, here]
                 high = weighted.astype(BF16)
-                parts[s * rows : (s + 1) * rows, :size] = high
-                parts[s * rows : (s + 1) * rows, size:] = (weighted - high.astype(F32)).astype(BF16)
+                parts[s * rows : (s + 1) * rows] = high
+                parts[size + s * rows : size + (s + 1) * rows] = (weighted - high.astype(F32)).astype(BF16)
             left = a_all[left_slot(a), :, here].reshape(size, size)
-            both = lax.dot_general(left, parts[...], (((0,), (0,)), ((), ())), preferred_element_type=F32)
-            out_acc[...] += both[:, :size] + both[:, size:]
+            twice = jnp.concatenate([left, left], axis=0)
+            out_acc[...] += lax.dot_general(twice, parts[...], (((0,), (0,)), ((), ())), preferred_element_type=F32)
 
     def take_env(chip, at_core, part, phase):
         a = chip // 2
@@ -424,7 +424,7 @@
             pltpu.VMEM((bonds, size, size), BF16),
             pltpu.VMEM((chips + side + 1, 2, size, size), BF16),
             pltpu.VMEM((side, 2, size, size), F32),
-            pltpu.VMEM((size, 2 * size), BF16),
+            pltpu.VMEM((2 * size, size), BF16),
             pltpu.VMEM((size, size), BF16),
             pltpu.VMEM((8, 128), F32),
             pltpu.VMEM((bonds, 8, 128), F32),

time: 139 us -> 139 us (level)
  no operation moved by 1% of the time
where the time goes in v5:
time: 139 us
  Pallas kernels  135 us (97%)
  between operations  2.97 us (2%)
    pallas_call x1, Pallas kernels, body(): pl.pallas_call(functools.partial(kernel, side, bonds, segs), out_shape=(p...  135 us

profile of v5, /device:TPU:7, one launch (start us, length us, event | category | flops | bytes accessed | tf_op | source)
XLA Modules:
  0.0 138.8 jit_solution(16669541290368035180)
XLA Ops:
  1.3 134.7 %shard_map.68 = (f32[1,1,512,512]{3,2,1,0:T(8,128)S(1)}, f32[1]{0:T(128)}) custom-call(s32[1,4]{1,0:T(1,128)} %ids.1, s32[1]{0:T(128)S(6)} %copy.8.counts, bf16[1,1,512,512]{3,2,1,0:T(8,128)(2,1)} %env.1, bf16[1,1,2,512,512]{4,3,2,1,0:T(8,128)(2,1)} %site.1, bf16[1,1,512,512]{3,2,1,0:T(8,128)(2,1)} %right.1), custom_call_target="tpu_custom_call" | custom-call | flops 25999998976 | bytes 6291456 | tf_op jit(solution)/shard_map/pallas_call | solution.py:415
  136.0 1.1 broadcast_multiply_fusion
